TPU v7x, 32 devices: a whole 2x2x4 slice. The times are simulated.
32 devices in a mesh: tile: 16 (over z, x, core), grp: 2 (over y).
Axes of the slice: x: 2, y: 2, z: 4, core: 2. Of those that a mesh axis runs over, the one named last changes fastest.
Arguments:
- snapshots: float32 [64, 2, 5, 8192], P(None, 'grp', None, 'tile'), may hold values from -2000 to 2000, as said below
- neighbors: int32 [8, 8192], P(None, 'tile'), may hold values from 0 to 767, as said below
- weights: float32 [8, 8192], P(None, 'tile'), may hold values from 0.02 to 0.14
- coupling: float32 [2, 2], replicated, may hold values from -4 to 4
Outputs:
- basis: float32 [64, 2, 5, 8192], P(None, 'grp', None, 'tile')
- coupled: float32 [64, 2, 5, 8192], P(None, 'grp', None, 'tile')
Inputs may be any that keep to these rules, and one draw needn't show every extreme that they name: `snapshots`: snapshot values of any sign. `neighbors`: each entry lies within 128 cells of its own cell in the extended block; entry 0 of every cell is the cell 128 before it and entry 1 the cell 128 after it.
All inputs are finite; a program needn't handle non-finite values.
Results may differ from a plain program's by a relative error of at most 0.0055.
Values may be sent and summed in bfloat16 or wider, within the bound.
A program may use at most 64 MiB of HBM per device.

v0:
```python
import jax
import jax.numpy as jnp
from jax import lax
from jax.sharding import PartitionSpec as P

HALO = 128


def padded(shard, sides, width):
    for axis, dim in sides:
        count, length = (lax.axis_size(axis), shard.shape[dim])
        up = [(i, (i + 1) % count) for i in range(count)]
        down = [(j, i) for i, j in up]
        last = lax.slice_in_dim(shard, length - width, length, axis=dim)
        leading = lax.slice_in_dim(shard, 0, width, axis=dim)
        before = lax.ppermute(last, axis, up)
        after = lax.ppermute(leading, axis, down)
        shard = jnp.concatenate([before, shard, after], axis=dim)
    return shard


def local(snapshots, neighbors, weights, coupling):
    snaps_count = snapshots.shape[0]
    extended = padded(snapshots, (("tile", 3),), HALO)
    ext_cells = extended.shape[3]
    cell_major = extended.reshape(-1, ext_cells).T
    stencil = jnp.zeros((snapshots.shape[3], cell_major.shape[1]), jnp.float32)
    for slot in range(neighbors.shape[0]):
        picked = jnp.take(cell_major, neighbors[slot], axis=0)
        stencil = stencil + weights[slot][:, None] * picked
    residual = snapshots - stencil.T.reshape(snapshots.shape)
    rows_all = float(residual.size // snaps_count * lax.axis_size("tile") * lax.axis_size("grp"))
    flat_rows = residual.reshape(snaps_count, -1)
    local_gram = jnp.dot(flat_rows, flat_rows.T, precision=lax.Precision.HIGHEST) / rows_all
    gram = lax.psum(local_gram, ("tile", "grp"))
    lower = jnp.linalg.cholesky(gram)
    inverse = jax.scipy.linalg.solve_triangular(
        lower, jnp.eye(snaps_count, dtype=jnp.float32), lower=True
    )
    instance = lax.axis_index("grp")
    coupling_row = lax.dynamic_slice_in_dim(coupling, instance, 1, 0)
    basis = jnp.dot(inverse, flat_rows, precision=lax.Precision.HIGHEST).reshape(residual.shape)
    rounded = basis.astype(jnp.bfloat16)
    own_rounded = rounded.astype(jnp.float32)
    mixed = jnp.einsum(
        "nm,kmfc->knfc",
        coupling_row,
        lax.all_gather(rounded, "grp", axis=1, tiled=True).astype(jnp.float32),
        precision=lax.Precision.HIGHEST,
    )
    return (basis, own_rounded + mixed)


def solution(mesh):
    return jax.shard_map(
        local,
        mesh=mesh,
        in_specs=(P(None, "grp", None, "tile"), P(None, "tile"), P(None, "tile"), P()),
        out_specs=(P(None, "grp", None, "tile"), P(None, "grp", None, "tile")),
        check_vma=False,
    )
```

profile of v0, /device:TPU:0, one launch (start us, length us, event | category | flops | bytes accessed | tf_op | source)
XLA Modules:
  0.0 106.5 jit_solution(5770573874695233273)
XLA Ops:
  0.6 0.0 copy-start
  0.6 0.0 copy-start.1
  0.7 1.2 %fusion.19 = (f32[64,1,5,128]{3,1,2,0:T(1,128)S(1)}, f32[64,1,5,128]{3,1,2,0:T(1,128)S(1)}) fusion(f32[64,1,5,512]{3,1,2,0:T(1,128)} %param.6), kind=kLoop, calls=%fused_computation.71 | loop fusion | bytes 655360 | tf_op jit(solution)/shard_map/slice | solution.py:14
  1.8 0.5 collective-permute-start
  2.3 5.0 %collective-permute-start.1 = (f32[64,1,5,128]{3,1,2,0:T(1,128)S(1)}, f32[64,1,5,128]{3,1,2,0:T(1,128)S(1)}, u32[]{:S(2)}, u32[]{:S(2)}) collective-permute-start(f32[64,1,5,128]{3,1,2,0:T(1,128)S(1)} %get-tuple-element.12), channel_id=1, source_target_pairs={{2,0},{4,2},{6,4},{8,6},{10,8},{12,10},{14,12},{16,14},{18,16},{20... | collective-permute-start | bytes 491528 | tf_op jit(solution)/shard_map/ppermute | solution.py:17
  7.3 1.0 fusion.21
  8.6 1.0 fusion.20
  9.7 0.7 collective-permute-done
  10.4 0.0 collective-permute-done.1
  10.4 0.0 copy-done.1
  10.4 2.8 %maximum_reduce_fusion = f32[64,5,768]{2,1,0:T(8,128)S(1)} fusion(f32[64,1,5,128]{3,1,2,0:T(1,128)S(1)} %collective-permute-done.1, f32[64,1,5,512]{3,1,2,0:T(1,128)S(1)} %copy-done.1, f32[64,1,5,128]{3,1,2,0:T(1,128)S(1)} %collective-permute-done), kind=kLoop, calls=%fused_computation.13 | loop fusion | flops 491520 | bytes 1966080 | tf_op jit(solution)/shard_map/concatenate | solution.py:18
  13.2 0.2 reshape.65
  13.3 0.4 copy.31
  13.7 1.6 %gather_fusion.2 = f32[512,320]{1,0:T(8,128)S(1)} fusion(f32[768,320]{1,0:T(8,128)S(1)} %bitcast.54, s32[1024]{0:T(1024)S(1)} %pad_clamp_fusion.5), kind=kCustom, calls=%fused_computation.2.clone | custom fusion | bytes 1312768 | tf_op jit(solution)/shard_map/jit(_take)/gather | solution.py:29
  15.3 2.3 %gather_fusion.3 = f32[512,320]{1,0:T(8,128)} fusion(f32[768,320]{1,0:T(8,128)S(1)} %bitcast.55, s32[1024]{0:T(1024)S(1)} %pad_clamp_fusion.4), kind=kCustom, calls=%fused_computation.3.clone | custom fusion | bytes 1312768 | tf_op jit(solution)/shard_map/jit(_take)/gather | solution.py:29
  17.6 2.3 %gather_fusion.4 = f32[512,320]{1,0:T(8,128)} fusion(f32[768,320]{1,0:T(8,128)S(1)} %bitcast.56, s32[1024]{0:T(1024)S(1)} %pad_clamp_fusion.3), kind=kCustom, calls=%fused_computation.4.clone | custom fusion | bytes 1312768 | tf_op jit(solution)/shard_map/jit(_take)/gather | solution.py:29
  19.9 2.3 %gather_fusion.5 = f32[512,320]{1,0:T(8,128)} fusion(f32[768,320]{1,0:T(8,128)S(1)} %bitcast.57, s32[1024]{0:T(1024)S(1)} %pad_clamp_fusion.2), kind=kCustom, calls=%fused_computation.5.clone | custom fusion | bytes 1312768 | tf_op jit(solution)/shard_map/jit(_take)/gather | solution.py:29
  22.2 2.3 %gather_fusion.6 = f32[512,320]{1,0:T(8,128)} fusion(f32[768,320]{1,0:T(8,128)S(1)} %bitcast.58, s32[1024]{0:T(1024)S(1)} %pad_clamp_fusion.1), kind=kCustom, calls=%fused_computation.6.clone | custom fusion | bytes 1312768 | tf_op jit(solution)/shard_map/jit(_take)/gather | solution.py:29
  24.5 2.3 %gather_fusion.7 = f32[512,320]{1,0:T(8,128)} fusion(f32[768,320]{1,0:T(8,128)S(1)} %bitcast.59, s32[1024]{0:T(1024)S(1)} %pad_clamp_fusion), kind=kCustom, calls=%fused_computation.7.clone | custom fusion | bytes 1312768 | tf_op jit(solution)/shard_map/jit(_take)/gather | solution.py:29
  26.8 2.3 %gather_fusion = f32[512,320]{1,0:T(8,128)} fusion(f32[768,320]{1,0:T(8,128)S(1)} %bitcast.60, s32[1024]{0:T(1024)S(1)} %pad_clamp_fusion.7), kind=kCustom, calls=%fused_computation.clone | custom fusion | bytes 1312768 | tf_op jit(solution)/shard_map/jit(_take)/gather | solution.py:29
  29.1 2.3 %gather_fusion.1 = f32[512,320]{1,0:T(8,128)} fusion(f32[768,320]{1,0:T(8,128)S(1)} %bitcast.61, s32[1024]{0:T(1024)S(1)} %pad_clamp_fusion.6), kind=kCustom, calls=%fused_computation.1.clone | custom fusion | bytes 1312768 | tf_op jit(solution)/shard_map/jit(_take)/gather | solution.py:29
  31.3 4.0 %fusion.3 = f32[320,512]{0,1:T(8,128)S(1)} fusion(f32[512,320]{1,0:T(8,128)} %gather_fusion.7, f32[512,320]{1,0:T(8,128)} %gather_fusion.6, f32[512,320]{1,0:T(8,128)} %gather_fusion.5, f32[512,320]{1,0:T(8,128)} %gather_fusion.4, f32[512,320]{1,0:T(8,128)} %gather_fusion.3, f32[512,320]{1,0:T(8,128)S(1)} %gather_fusion.2, f32[512,320]{1,0:T(8,128)} %gather_fusion.1, ...), kind=kLoop, calls=%fused_computation.16 | loop fusion | flops 3768320 | bytes 5918720 | tf_op jit(solution)/shard_map/transpose | solution.py:31
  35.4 0.2 copy.32
  35.6 0.1 reshape.66
  35.7 0.2 copy_subtract_fusion
  35.9 1.3 %fusion = f32[64,64]{0,1:T(8,128)S(1)} fusion(f32[64,1,5,512]{3,2,0,1:T(8,128)S(1)} %copy_subtract_fusion), kind=kOutput, calls=%fused_computation.9 | convolution fusion | flops 125833216 | bytes 671744 | tf_op jit(solution)/shard_map/dot_general | solution.py:34
  37.2 0.4 copy.49
  37.6 39.6 %psum.7 = f32[64,64]{0,1:T(8,128)S(1)} all-reduce(f32[64,64]{0,1:T(8,128)S(1)} %fusion), channel_id=1, replica_groups=mesh['tile'=16,'grp'=2] {'tile','grp'}, use_global_device_ids=true, to_apply=%region_0.0 | all-reduce | flops 4096 | bytes 32768 | tf_op jit(solution)/shard_map/psum | solution.py:35
  77.3 0.1 copy.36
  77.4 5.8 %cholesky.17 = f32[64,64]{1,0:T(8,128)S(1)} custom-call(f32[64,64]{1,0:T(8,128)S(1)} %fusion.17), custom_call_target="Cholesky" | custom-call | tf_op jit(solution)/shard_map/jit(cholesky)/cholesky | solution.py:36
  83.2 0.6 compare_reduce_fusion
  83.9 0.7 fusion.14
  84.6 4.9 %custom-call.7 = f32[1,64,64]{1,2,0:T(8,128)S(1)} custom-call(f32[1,64,64]{2,1,0:T(8,128)S(1)} %fusion.14), custom_call_target="InvertDiagBlocksLowerTriangular" | custom-call | tf_op jit(solution)/shard_map/jit(_solve_triangular)/triangular_solve | solution.py:37
  89.4 0.2 fusion.15
  89.7 0.7 convert_convert_fusion
  90.4 0.3 reshape.69
  90.7 0.1 convert_element_type.26
  90.8 1.5 %copy.39 = f32[64,1,5,512]{3,1,2,0:T(1,128)} copy(f32[64,1,5,512]{3,2,0,1:T(8,128)S(1)} %reshape.69) | data formatting | bytes 1310720
  92.3 0.1 copy.37
  92.4 9.9 %all_gather.3 = bf16[64,2,5,512]{3,0,2,1:T(8,128)(2,1)S(1)} all-gather(bf16[64,1,5,512]{3,0,2,1:T(8,128)(2,1)S(1)} %copy.37), channel_id=1, replica_groups=mesh['tile'=16,'grp'=2] {'grp'}, dimensions={1}, use_global_device_ids=true | all-gather | bytes 983040 | tf_op jit(solution)/shard_map/all_gather | solution.py:48
  102.3 0.3 reshape.71
  102.6 0.0 copy-done
  102.6 2.2 %fusion.12 = f32[1,64,5,512]{3,0,2,1:T(1,128)S(1)} fusion(bf16[64,2,5,512]{3,0,2,1:T(8,128)(2,1)S(1)} %all_gather.3, f32[2,2]{1,0:T(2,128)S(1)} %copy-done, s32[]{:T(128)S(6)} %select_n.15), kind=kOutput, calls=%fused_computation.32 | convolution fusion | flops 3932160 | bytes 1311236 | tf_op jit(solution)/shard_map/nm,kmfc->knfc/dot_general | solution.py:45
  104.8 0.2 fusion.1
  105.0 1.5 %copy.40 = f32[64,1,5,512]{3,1,2,0:T(1,128)} copy(f32[64,1,5,512]{3,2,0,1:T(8,128)S(1)} %fusion.1) | data formatting | bytes 1310720
  (22 shorter events, 0.2 us)
Async XLA Ops:
  0.6 102.0 %copy-start = (f32[2,2]{1,0:T(2,128)S(1)}, f32[2,2]{1,0:T(2,128)}, u32[]{:S(2)}) copy-start(f32[2,2]{1,0:T(2,128)} %param.9) | copy-start | bytes 52
  0.6 9.8 %copy-start.1 = (f32[64,1,5,512]{3,1,2,0:T(1,128)S(1)}, f32[64,1,5,512]{3,1,2,0:T(1,128)}, u32[]{:S(2)}) copy-start(f32[64,1,5,512]{3,1,2,0:T(1,128)} %param.6) | copy-start | bytes 1966084
  1.8 8.6 %collective-permute-start = (f32[64,1,5,128]{3,1,2,0:T(1,128)S(1)}, f32[64,1,5,128]{3,1,2,0:T(1,128)S(1)}, u32[]{:S(2)}, u32[]{:S(2)}) collective-permute-start(f32[64,1,5,128]{3,1,2,0:T(1,128)S(1)} %get-tuple-element.11), channel_id=1, source_target_pairs={{0,2},{2,4},{4,6},{6,8},{8,10},{10,12},{12,14},{14,16},{16,18},{18... | collective-permute-start | bytes 491528 | tf_op jit(solution)/shard_map/ppermute | solution.py:16
  2.3 8.1 %collective-permute-start.1 = (f32[64,1,5,128]{3,1,2,0:T(1,128)S(1)}, f32[64,1,5,128]{3,1,2,0:T(1,128)S(1)}, u32[]{:S(2)}, u32[]{:S(2)}) collective-permute-start(f32[64,1,5,128]{3,1,2,0:T(1,128)S(1)} %get-tuple-element.12), channel_id=1, source_target_pairs={{2,0},{4,2},{6,4},{8,6},{10,8},{12,10},{14,12},{16,14},{18,16},{20... | collective-permute-start | bytes 491528 | tf_op jit(solution)/shard_map/ppermute | solution.py:17
where the time goes:
time: 107 us
  blocking collectives  49.5 us (46%)
  local copies, waits for them, and re-layouts  26 us (24%)
  other arithmetic  19.4 us (18%)
  starting transfers between devices  5.53 us (5%)
  matrix products  4.41 us (4%)
    psum x1, blocking collectives, local(): gram = lax.psum(local_gram, ('tile', 'grp'))  39.6 us
    gather x8, local copies, waits for them, and re-layouts, local(): picked = jnp.take(cell_major, neighbors[slot], axis=0)  17.6 us
    all_gather x1, blocking collectives, local(): lax.all_gather(rounded, 'grp', axis=1, tiled=True).astype(jnp.float32)  9.85 us
    another operation x3, other arithmetic, local(): lower = jnp.linalg.cholesky(gram)  6.52 us
    another operation x2, other arithmetic, local(): jax.scipy.linalg.solve_triangular(lower, jnp.eye(snaps_count, dtype=jnp.f...  5.55 us
    ppermute x1, starting transfers between devices, padded(): after = lax.ppermute(leading, axis, down)  5.03 us
    transpose x1, other arithmetic, local(): residual = snapshots - stencil.T.reshape(snapshots.shape)  4.02 us
    unnamed x7, local copies, waits for them, and re-layouts  3.42 us
  transfers between devices with their start and end apart: 2, of which 1 were waited for; matrix products, arithmetic and copies ran while one was open for 2% of the time, Pallas kernels for 0%

commit v1 on v0

v1 whole, which is shorter than its diff:
```python
import functools

import jax
import jax.numpy as jnp
from jax import lax
from jax.experimental import pallas as pl
from jax.experimental.pallas import tpu as pltpu
from jax.sharding import PartitionSpec as P

HALO = 128
LANES = 128
MESH = pl.DeviceIdType.MESH
F32 = jnp.float32
BF16 = jnp.bfloat16


def split(value):
    high = value.astype(BF16)
    return high, (value - high.astype(F32)).astype(BF16)


def inverse_factor(gram):
    n = gram.shape[0]
    rows = lax.broadcasted_iota(jnp.int32, (n, n), 0)
    cols = lax.broadcasted_iota(jnp.int32, (n, n), 1)
    both = jnp.concatenate([gram, jnp.where(rows == cols, 1.0, 0.0).astype(F32)], axis=1)
    blocks = [both[8 * b:8 * b + 8] for b in range(n // 8)]
    sub = lax.broadcasted_iota(jnp.int32, (8, 2 * n), 0)
    lane = lax.broadcasted_iota(jnp.int32, (8, 2 * n), 1)
    for j in range(n):
        b, r = divmod(j, 8)
        row = jnp.broadcast_to(blocks[b][r:r + 1], (8, 2 * n))
        inv = 1.0 / jnp.broadcast_to(row[:, j:j + 1], (8, 2 * n))
        scaled = row * inv
        for bb in range(b, n // 8):
            factor = jnp.broadcast_to(blocks[bb][:, j:j + 1], (8, 2 * n))
            if bb == b:
                factor = jnp.where(sub > r, factor, 0.0)
            blocks[bb] = blocks[bb] - factor * scaled
    out = []
    for b in range(n // 8):
        pivot = jnp.sum(jnp.where(lane == sub + 8 * b, blocks[b], 0.0), axis=1, keepdims=True)
        out.append(blocks[b] * lax.rsqrt(pivot))
    return jnp.concatenate(out, axis=0)[:, n:]


def reduce_kernel(dims, x_ref, nbr_ref, w_ref, res_ref, other_ref, inv_ref,
                  edge, halo, stencil, resbf, gsend, grecv, tsend, trecv,
                  hs, hr, s1, r1, s2, r2, s3, r3):
    tiles, grps, low, snaps, fields, chunks = dims
    n1, n2 = low * grps, tiles // low
    me_t, me_g = lax.axis_index("tile"), lax.axis_index("grp")
    right, left = lax.rem(me_t + 1, tiles), lax.rem(me_t + tiles - 1, tiles)
    base, me_low = (me_t // low) * low, lax.rem(me_t, low)
    me1, me2 = me_low * grps + me_g, me_t // low

    def near(d):
        to = lax.rem(me1 + d, n1)
        return (base + to // grps, lax.rem(to, grps))

    def far(d):
        return (lax.rem(me2 + d, n2) * low + me_low, me_g)

    barrier = pltpu.get_barrier_semaphore()
    partners = [(left, me_g), (right, me_g)] + [near(d) for d in range(1, n1)] + [far(d) for d in range(1, n2)]
    for partner in partners:
        pl.semaphore_signal(barrier, inc=1, device_id=partner, device_id_type=MESH)

    step = fields * chunks

    def chunk(q):
        return jnp.concatenate(
            [x_ref[pl.ds(f * chunks + q, snaps, stride=step), :] for f in range(fields)], axis=0)

    edge[0] = chunk(chunks - 1).astype(BF16)
    edge[1] = chunk(0).astype(BF16)
    pl.semaphore_wait(barrier, len(partners))
    sends = []
    for side, to in ((0, right), (1, left)):
        copy = pltpu.make_async_remote_copy(
            src_ref=edge.at[side], dst_ref=halo.at[side], send_sem=hs.at[side], recv_sem=hr.at[side],
            device_id=(to, me_g), device_id_type=MESH)
        copy.start()
        sends.append(copy)

    iota = lax.broadcasted_iota(jnp.int32, (3 * LANES, LANES), 0)
    for q in range(chunks):
        here = slice(q * LANES, (q + 1) * LANES)
        total = jnp.zeros((3 * LANES, LANES), F32)
        for j in range(nbr_ref.shape[0]):
            total = total + jnp.where(iota == nbr_ref[j:j + 1, here] - q * LANES, w_ref[j:j + 1, here], 0.0)
        stencil[q] = total.astype(BF16)

    own = [chunk(q).astype(BF16) for q in range(chunks)]

    def part(q, d, block):
        return jnp.dot(block, stencil[q, d * LANES:(d + 1) * LANES, :], preferred_element_type=F32)

    sums = []
    for q in range(chunks):
        total = None
        for d in range(3):
            if 0 <= q + d - 1 < chunks:
                term = part(q, d, own[q + d - 1])
                total = term if total is None else total + term
        sums.append(total)
    for copy in sends:
        copy.wait()
    sums[0] = sums[0] + part(0, 0, halo[0])
    sums[-1] = sums[-1] + part(chunks - 1, 2, halo[1])
    highs, lows = [], []
    rows = snaps * fields
    for q in range(chunks):
        res = chunk(q) - sums[q]
        res_ref[q * rows:(q + 1) * rows, :] = res
        high, low_part = split(res)
        resbf[q * rows:(q + 1) * rows, :] = high
        highs.append(high)
        lows.append(low_part)

    gram = jnp.zeros((2 * snaps, snaps), F32)
    for f in range(fields):
        at = slice(f * snaps, (f + 1) * snaps)
        high = jnp.concatenate([h[at] for h in highs], axis=1)
        low_part = jnp.concatenate([h[at] for h in lows], axis=1)
        gram = gram + lax.dot_general(jnp.concatenate([high, low_part], axis=0), high,
                                      (((1,), (1,)), ((), ())), preferred_element_type=F32)
    gram = gram[:snaps] + (gram[snaps:] + gram[snaps:].T)
    gram = gram * (1.0 / (fields * chunks * LANES * tiles * grps))
    half = snaps // 2
    gsend[...] = jnp.concatenate([gram[:half], gram[half:]], axis=1)

    def exchange(count, where, src, dst, ss, rs):
        copies = []
        for d in range(1, count):
            copy = pltpu.make_async_remote_copy(
                src_ref=src, dst_ref=dst.at[d - 1], send_sem=ss.at[d - 1], recv_sem=rs.at[d - 1],
                device_id=where(d), device_id_type=MESH)
            copy.start()
            copies.append(copy)
        return copies

    copies = exchange(n1, near, gsend, grecv, s1, r1)
    total = gsend[...]
    for d, copy in enumerate(copies):
        copy.wait_recv()
        total = total + grecv[d]
    tsend[...] = total
    far_copies = exchange(n2, far, tsend, trecv, s2, r2)
    res_copies = exchange(grps, lambda d: (me_t, lax.rem(me_g + d, grps)), resbf, other_ref, s3, r3)
    for d, copy in enumerate(far_copies):
        copy.wait_recv()
        total = total + trecv[d]
    gram = jnp.concatenate([total[:, :snaps], total[:, snaps:]], axis=0)
    inv_ref[...] = inverse_factor(gram)
    for copy in copies + far_copies:
        copy.wait_send()
    for copy in res_copies:
        copy.wait()


def basis_kernel(dims, inv_ref, res_ref, other_ref, coupling_ref, basis_ref, coupled_ref):
    tiles, grps, low, snaps, fields, chunks = dims
    me_g = lax.axis_index("grp")
    rows, step = snaps * fields, fields * chunks
    high, low_part = split(inv_ref[...])
    three = jnp.concatenate([high, low_part, high], axis=1)
    two = jnp.concatenate([high, low_part], axis=1)
    own_scale = coupling_ref[me_g, me_g]
    scales = [coupling_ref[me_g, lax.rem(me_g + grps - d, grps)] for d in range(1, grps)]
    for f in range(fields):
        for q in range(chunks):
            at = pl.ds(q * rows + f * snaps, snaps)
            to = pl.ds(f * chunks + q, snaps, stride=step)
            rh, rl = split(res_ref[at, :])
            basis = jnp.dot(three, jnp.concatenate([rh, rh, rl], axis=0), preferred_element_type=F32)
            basis_ref[to, :] = basis
            rounded = basis.astype(BF16).astype(F32)
            mixed = own_scale * rounded
            for d in range(1, grps):
                there = other_ref[d - 1, at, :]
                theirs = jnp.dot(two, jnp.concatenate([there, there], axis=0), preferred_element_type=F32)
                mixed = mixed + scales[d - 1] * theirs.astype(BF16).astype(F32)
            coupled_ref[to, :] = rounded + mixed


def local(mesh, snapshots, neighbors, weights, coupling):
    tiles, grps = mesh.shape["tile"], mesh.shape["grp"]
    snaps, _, fields, cells = snapshots.shape
    chunks = cells // LANES
    low = 4
    dims = (tiles, grps, low, snaps, fields, chunks)
    n1, n2 = low * grps, tiles // low
    rows = snaps * fields
    count = rows * chunks
    x = snapshots.reshape(count, LANES)
    vmem = pl.BlockSpec(memory_space=pltpu.VMEM)
    dma = lambda n: pltpu.SemaphoreType.DMA((n,))
    res, other, inverse = pl.pallas_call(
        functools.partial(reduce_kernel, dims),
        out_shape=(jax.ShapeDtypeStruct((count, LANES), F32),
                   jax.ShapeDtypeStruct((grps - 1, count, LANES), BF16),
                   jax.ShapeDtypeStruct((snaps, snaps), F32)),
        in_specs=[vmem] * 3,
        out_specs=(vmem,) * 3,
        scratch_shapes=[
            pltpu.VMEM((2, rows, LANES), BF16),
            pltpu.VMEM((2, rows, LANES), BF16),
            pltpu.VMEM((chunks, 3 * LANES, LANES), BF16),
            pltpu.VMEM((count, LANES), BF16),
            pltpu.VMEM((snaps // 2, 2 * snaps), F32),
            pltpu.VMEM((n1 - 1, snaps // 2, 2 * snaps), F32),
            pltpu.VMEM((snaps // 2, 2 * snaps), F32),
            pltpu.VMEM((n2 - 1, snaps // 2, 2 * snaps), F32),
            dma(2), dma(2), dma(n1 - 1), dma(n1 - 1), dma(n2 - 1), dma(n2 - 1), dma(grps - 1), dma(grps - 1),
        ],
        compiler_params=pltpu.CompilerParams(
            collective_id=0, has_side_effects=True, vmem_limit_bytes=32 * 2 ** 20),
        name="reduce",
    )(x, neighbors, weights)
    basis, coupled = pl.pallas_call(
        functools.partial(basis_kernel, dims),
        out_shape=(jax.ShapeDtypeStruct((count, LANES), F32),) * 2,
        in_specs=[vmem] * 3 + [pl.BlockSpec(memory_space=pltpu.SMEM)],
        out_specs=(vmem,) * 2,
        compiler_params=pltpu.CompilerParams(vmem_limit_bytes=32 * 2 ** 20),
        name="basis",
    )(inverse, res, other, coupling)
    return basis.reshape(snapshots.shape), coupled.reshape(snapshots.shape)


def solution(mesh):
    return jax.shard_map(
        functools.partial(local, mesh),
        mesh=mesh,
        in_specs=(P(None, "grp", None, "tile"), P(None, "tile"), P(None, "tile"), P()),
        out_specs=(P(None, "grp", None, "tile"), P(None, "grp", None, "tile")),
        check_vma=False,
    )
```

time: 107 us -> 32.7 us (0.31)
  blocking collectives: 49.5 us -> 0 us
  Pallas kernels: 0 us -> 28.5 us
  local copies, waits for them, and re-layouts: 26 us -> 3.19 us
  other arithmetic: 19.4 us -> 0 us
  starting transfers between devices: 5.53 us -> 0 us
  matrix products: 4.41 us -> 0 us
    psum x1 -> x0, blocking collectives: 39.6 us -> none  [local(): gram = lax.psum(local_gram, ('tile', 'grp'))]
    pallas_call x0 -> x2, Pallas kernels: none -> 28.5 us  [the longest x1 26.2 us: local(): pl.pallas_call(functools.partial(reduce_kernel, dims), out_shape=(jax.Sha...]
    gather x8 -> x0, local copies, waits for them, and re-layouts: 17.6 us -> none  [local(): picked = jnp.take(cell_major, neighbors[slot], axis=0)]
    another operation x5 -> x0, other arithmetic: 12.1 us -> none  [the longest x3 6.52 us: local(): lower = jnp.linalg.cholesky(gram)]
    all_gather x1 -> x0, blocking collectives: 9.85 us -> none  [local(): lax.all_gather(rounded, 'grp', axis=1, tiled=True).astype(jnp.float32)]
    ppermute x2 -> x0, starting transfers between devices: 5.53 us -> none  [the longest x1 5.03 us: padded(): after = lax.ppermute(leading, axis, down)]
    dot_general x3 -> x0, matrix products: 4.18 us -> none  [the longest x1 2.2 us: local(): jnp.einsum('nm,kmfc->knfc', coupling_row, lax.all_gather(rounded, 'grp',...]
    transpose x1 -> x0, other arithmetic: 4.02 us -> none  [local(): residual = snapshots - stencil.T.reshape(snapshots.shape)]
  transfers between devices with their start and end apart: 2 -> 0, of which waited for: 1 -> 0; matrix products, arithmetic and copies ran while one was open for 2% -> 0% of each run, Pallas kernels for 0% -> 0%
where the time goes in v1:
time: 32.7 us; the launch traced here: 32.3 us
  Pallas kernels  28.5 us (87%)
  local copies, waits for them, and re-layouts  3.19 us (10%)
  between operations  0.66 us (2%)
    pallas_call x1, Pallas kernels, local(): pl.pallas_call(functools.partial(reduce_kernel, dims), out_shape=(jax.Sha...  26.2 us
    unnamed x8, local copies, waits for them, and re-layouts  3.19 us
    pallas_call x1, Pallas kernels, local(): pl.pallas_call(functools.partial(basis_kernel, dims), out_shape=(jax.Shap...  2.24 us

profile of v1, /device:TPU:0, one launch (start us, length us, event | category | flops | bytes accessed | tf_op | source)
XLA Modules:
  0.0 32.3 jit_solution(14627564347003099257)
XLA Ops:
  0.6 0.0 copy-start
  0.6 1.1 %copy-done = f32[64,1,5,512]{3,1,2,0:T(1,128)S(1)} copy-done((f32[64,1,5,512]{3,1,2,0:T(1,128)S(1)}, f32[64,1,5,512]{3,1,2,0:T(1,128)}, u32[]{:S(2)}) %copy-start) | copy-done | bytes 655384
  1.7 0.0 copy-start.1
  1.7 0.7 %copy-done.1 = s32[8,512]{1,0:T(8,128)S(1)} copy-done((s32[8,512]{1,0:T(8,128)S(1)}, s32[8,512]{1,0:T(8,128)}, u32[]{:S(2)}) %copy-start.1) | copy-done | bytes 16408
  2.4 0.0 copy-start.2
  2.4 0.7 %copy-done.2 = f32[8,512]{1,0:T(8,128)S(1)} copy-done((f32[8,512]{1,0:T(8,128)S(1)}, f32[8,512]{1,0:T(8,128)}, u32[]{:S(2)}) %copy-start.2) | copy-done | bytes 16408
  3.2 26.2 %reduce.1 = (f32[1280,128]{1,0:T(8,128)S(1)}, bf16[1,1280,128]{2,1,0:T(8,128)(2,1)S(1)}, f32[64,64]{1,0:T(8,128)S(1)}) custom-call(f32[1280,128]{1,0:T(8,128)S(1)} %bitcast.3, s32[8,512]{1,0:T(8,128)S(1)} %copy-done.1, f32[8,512]{1,0:T(8,128)S(1)} %copy-done.2), custom_call_target="tpu_custom_call" | custom-call | tf_op jit(solution)/shard_map/reduce/pallas_call | solution.py:199
  29.4 0.0 copy-start.3
  29.4 0.7 %copy-done.3 = f32[2,2]{1,0:T(2,128)S(1)} copy-done((f32[2,2]{1,0:T(2,128)S(1)}, f32[2,2]{1,0:T(2,128)}, u32[]{:S(2)}) %copy-start.3) | copy-done | bytes 40
  30.1 2.2 %basis.1 = (f32[1280,128]{1,0:T(8,128)}, f32[1280,128]{1,0:T(8,128)}) custom-call(f32[64,64]{1,0:T(8,128)S(1)} %get-tuple-element.7.inv_ref, f32[1280,128]{1,0:T(8,128)S(1)} %get-tuple-element.8.res_ref, bf16[1,1280,128]{2,1,0:T(8,128)(2,1)S(1)} %get-tuple-element.9.other_ref, f32[2,2]{1,0:T(2,128)S(1)} %copy-done.3), custom_call_target="tpu_custom_call" | custom-call | tf_op jit(solution)/shard_map/basis/pallas_call | solution.py:221
Async XLA Ops:
  0.6 1.1 %copy-start = (f32[64,1,5,512]{3,1,2,0:T(1,128)S(1)}, f32[64,1,5,512]{3,1,2,0:T(1,128)}, u32[]{:S(2)}) copy-start(f32[64,1,5,512]{3,1,2,0:T(1,128)} %param.4) | copy-start | bytes 1966084
  1.7 0.7 %copy-start.1 = (s32[8,512]{1,0:T(8,128)S(1)}, s32[8,512]{1,0:T(8,128)}, u32[]{:S(2)}) copy-start(s32[8,512]{1,0:T(8,128)} %nbr_ref.1) | copy-start | bytes 49156
  2.4 0.7 %copy-start.2 = (f32[8,512]{1,0:T(8,128)S(1)}, f32[8,512]{1,0:T(8,128)}, u32[]{:S(2)}) copy-start(f32[8,512]{1,0:T(8,128)} %w_ref.1) | copy-start | bytes 49156
  29.4 0.7 %copy-start.3 = (f32[2,2]{1,0:T(2,128)S(1)}, f32[2,2]{1,0:T(2,128)}, u32[]{:S(2)}) copy-start(f32[2,2]{1,0:T(2,128)} %coupling_ref.1) | copy-start | bytes 52

commit v2 on v1

--- a/solution.py
+++ b/solution.py
@@ -20,33 +20,48 @@
 
 
 def inverse_factor(gram):
-    n = gram.shape[0]
+    n, p = gram.shape[0], 8
+    w = 2 * n
     rows = lax.broadcasted_iota(jnp.int32, (n, n), 0)
     cols = lax.broadcasted_iota(jnp.int32, (n, n), 1)
     both = jnp.concatenate([gram, jnp.where(rows == cols, 1.0, 0.0).astype(F32)], axis=1)
-    blocks = [both[8 * b:8 * b + 8] for b in range(n // 8)]
-    sub = lax.broadcasted_iota(jnp.int32, (8, 2 * n), 0)
-    lane = lax.broadcasted_iota(jnp.int32, (8, 2 * n), 1)
-    for j in range(n):
-        b, r = divmod(j, 8)
-        row = jnp.broadcast_to(blocks[b][r:r + 1], (8, 2 * n))
-        inv = 1.0 / jnp.broadcast_to(row[:, j:j + 1], (8, 2 * n))
-        scaled = row * inv
-        for bb in range(b, n // 8):
-            factor = jnp.broadcast_to(blocks[bb][:, j:j + 1], (8, 2 * n))
-            if bb == b:
-                factor = jnp.where(sub > r, factor, 0.0)
-            blocks[bb] = blocks[bb] - factor * scaled
+    blocks = [both[p * b:p * b + p] for b in range(n // p)]
+    sub = lax.broadcasted_iota(jnp.int32, (p, w), 0)
+
+    def full(value):
+        return jnp.broadcast_to(value, (p, w))
+
     out = []
-    for b in range(n // 8):
-        pivot = jnp.sum(jnp.where(lane == sub + 8 * b, blocks[b], 0.0), axis=1, keepdims=True)
-        out.append(blocks[b] * lax.rsqrt(pivot))
+    for b in range(n // p):
+        c = p * b
+        row = [full(blocks[b][r:r + 1]) for r in range(p)]
+        a = {(r, s): full(row[r][:, c + s:c + s + 1]) for r in range(p) for s in range(r, p)}
+        inv = []
+        for r in range(p):
+            inv.append(1.0 / a[r, r])
+            for s in range(r + 1, p):
+                m = a[r, s] * inv[r]
+                row[s] = row[s] - m * row[r]
+                for t in range(s, p):
+                    a[s, t] = a[s, t] - m * a[r, t]
+        for bb in range(b + 1, n // p):
+            col = [full(blocks[bb][:, c + s:c + s + 1]) for s in range(p)]
+            for r in range(p):
+                factor = col[r] * inv[r]
+                for s in range(r + 1, p):
+                    col[s] = col[s] - factor * a[r, s]
+                blocks[bb] = blocks[bb] - factor * row[r]
+        done, pivot = row[0], a[0, 0]
+        for r in range(1, p):
+            done = jnp.where(sub == r, row[r], done)
+            pivot = jnp.where(sub == r, a[r, r], pivot)
+        out.append(done * lax.rsqrt(pivot))
     return jnp.concatenate(out, axis=0)[:, n:]
 
 
-def reduce_kernel(dims, x_ref, nbr_ref, w_ref, res_ref, other_ref, inv_ref,
-                  edge, halo, stencil, resbf, gsend, grecv, tsend, trecv,
-                  hs, hr, s1, r1, s2, r2, s3, r3):
+def reduce_kernel(dims, x_hbm, nbr_hbm, w_hbm, coupling_hbm, res_ref, other_ref, inv_ref, coupling_ref,
+                  x_ref, nbr_ref, w_ref, pairs, edge, halo, stencil, resbf, gsend, grecv, tsend, trecv,
+                  hs, hr, s1, r1, s2, r2, s3, r3, loads):
     tiles, grps, low, snaps, fields, chunks = dims
     n1, n2 = low * grps, tiles // low
     me_t, me_g = lax.axis_index("tile"), lax.axis_index("grp")
@@ -66,12 +81,27 @@
     for partner in partners:
         pl.semaphore_signal(barrier, inc=1, device_id=partner, device_id_type=MESH)
 
+    ins = [pltpu.make_async_copy(src, dst, loads.at[i]) for i, (src, dst) in enumerate(
+        ((x_hbm, x_ref), (nbr_hbm, nbr_ref), (w_hbm, w_ref), (coupling_hbm, pairs)))]
+    for copy in (ins[1], ins[2], ins[0], ins[3]):
+        copy.start()
     step = fields * chunks
 
     def chunk(q):
         return jnp.concatenate(
             [x_ref[pl.ds(f * chunks + q, snaps, stride=step), :] for f in range(fields)], axis=0)
 
+    ins[1].wait()
+    ins[2].wait()
+    iota = lax.broadcasted_iota(jnp.int32, (3 * LANES, LANES), 0)
+    for q in range(chunks):
+        here = slice(q * LANES, (q + 1) * LANES)
+        total = jnp.zeros((3 * LANES, LANES), F32)
+        for j in range(nbr_ref.shape[0]):
+            total = total + jnp.where(iota == nbr_ref[j:j + 1, here] - q * LANES, w_ref[j:j + 1, here], 0.0)
+        stencil[q] = total.astype(BF16)
+
+    ins[0].wait()
     edge[0] = chunk(chunks - 1).astype(BF16)
     edge[1] = chunk(0).astype(BF16)
     pl.semaphore_wait(barrier, len(partners))
@@ -82,14 +112,6 @@
             device_id=(to, me_g), device_id_type=MESH)
         copy.start()
         sends.append(copy)
-
-    iota = lax.broadcasted_iota(jnp.int32, (3 * LANES, LANES), 0)
-    for q in range(chunks):
-        here = slice(q * LANES, (q + 1) * LANES)
-        total = jnp.zeros((3 * LANES, LANES), F32)
-        for j in range(nbr_ref.shape[0]):
-            total = total + jnp.where(iota == nbr_ref[j:j + 1, here] - q * LANES, w_ref[j:j + 1, here], 0.0)
-        stencil[q] = total.astype(BF16)
 
     own = [chunk(q).astype(BF16) for q in range(chunks)]
 
@@ -153,6 +175,8 @@
         total = total + trecv[d]
     gram = jnp.concatenate([total[:, :snaps], total[:, snaps:]], axis=0)
     inv_ref[...] = inverse_factor(gram)
+    ins[3].wait()
+    coupling_ref[...] = pairs[...]
     for copy in copies + far_copies:
         copy.wait_send()
     for copy in res_copies:
@@ -166,8 +190,16 @@
     high, low_part = split(inv_ref[...])
     three = jnp.concatenate([high, low_part, high], axis=1)
     two = jnp.concatenate([high, low_part], axis=1)
-    own_scale = coupling_ref[me_g, me_g]
-    scales = [coupling_ref[me_g, lax.rem(me_g + grps - d, grps)] for d in range(1, grps)]
+    rows_at = lax.broadcasted_iota(jnp.int32, (grps, grps), 0)
+    cols_at = lax.broadcasted_iota(jnp.int32, (grps, grps), 1)
+
+    def scale(d):
+        here = (rows_at == me_g) & (cols_at == lax.rem(me_g + grps - d, grps))
+        kept = jnp.where(here, coupling_ref[...], 0.0)
+        return jnp.sum(jnp.sum(kept, axis=1, keepdims=True), axis=0, keepdims=True)
+
+    own_scale = scale(0)
+    scales = [scale(d) for d in range(1, grps)]
     for f in range(fields):
         for q in range(chunks):
             at = pl.ds(q * rows + f * snaps, snaps)
@@ -196,14 +228,19 @@
     x = snapshots.reshape(count, LANES)
     vmem = pl.BlockSpec(memory_space=pltpu.VMEM)
     dma = lambda n: pltpu.SemaphoreType.DMA((n,))
-    res, other, inverse = pl.pallas_call(
+    res, other, inverse, pairs = pl.pallas_call(
         functools.partial(reduce_kernel, dims),
         out_shape=(jax.ShapeDtypeStruct((count, LANES), F32),
                    jax.ShapeDtypeStruct((grps - 1, count, LANES), BF16),
-                   jax.ShapeDtypeStruct((snaps, snaps), F32)),
-        in_specs=[vmem] * 3,
-        out_specs=(vmem,) * 3,
+                   jax.ShapeDtypeStruct((snaps, snaps), F32),
+                   jax.ShapeDtypeStruct(coupling.shape, F32)),
+        in_specs=[pl.BlockSpec(memory_space=pltpu.HBM)] * 4,
+        out_specs=(vmem,) * 4,
         scratch_shapes=[
+            pltpu.VMEM((count, LANES), F32),
+            pltpu.VMEM(neighbors.shape, jnp.int32),
+            pltpu.VMEM(weights.shape, F32),
+            pltpu.VMEM(coupling.shape, F32),
             pltpu.VMEM((2, rows, LANES), BF16),
             pltpu.VMEM((2, rows, LANES), BF16),
             pltpu.VMEM((chunks, 3 * LANES, LANES), BF16),
@@ -213,19 +250,20 @@
             pltpu.VMEM((snaps // 2, 2 * snaps), F32),
             pltpu.VMEM((n2 - 1, snaps // 2, 2 * snaps), F32),
             dma(2), dma(2), dma(n1 - 1), dma(n1 - 1), dma(n2 - 1), dma(n2 - 1), dma(grps - 1), dma(grps - 1),
+            dma(4),
         ],
         compiler_params=pltpu.CompilerParams(
             collective_id=0, has_side_effects=True, vmem_limit_bytes=32 * 2 ** 20),
         name="reduce",
-    )(x, neighbors, weights)
+    )(*[pltpu.with_memory_space_constraint(a, pltpu.HBM) for a in (x, neighbors, weights, coupling)])
     basis, coupled = pl.pallas_call(
         functools.partial(basis_kernel, dims),
         out_shape=(jax.ShapeDtypeStruct((count, LANES), F32),) * 2,
-        in_specs=[vmem] * 3 + [pl.BlockSpec(memory_space=pltpu.SMEM)],
+        in_specs=[vmem] * 4,
         out_specs=(vmem,) * 2,
         compiler_params=pltpu.CompilerParams(vmem_limit_bytes=32 * 2 ** 20),
         name="basis",
-    )(inverse, res, other, coupling)
+    )(inverse, res, other, pairs)
     return basis.reshape(snapshots.shape), coupled.reshape(snapshots.shape)
 
 

time: 32.7 us -> 25.2 us (0.77)
  Pallas kernels: 28.5 us -> 24.3 us
  local copies, waits for them, and re-layouts: 3.19 us -> 0 us
    pallas_call x1, Pallas kernels: 26.2 us -> 22.6 us  [local(): pl.pallas_call(functools.partial(reduce_kernel, dims), out_shape=(jax.Sha...]
    unnamed x8 -> x0, local copies, waits for them, and re-layouts: 3.19 us -> none
    pallas_call x1, Pallas kernels: 2.24 us -> 1.69 us  [local(): pl.pallas_call(functools.partial(basis_kernel, dims), out_shape=(jax.Shap...]
where the time goes in v2:
time: 25.2 us; the launch traced here: 25 us
  Pallas kernels  24.3 us (96%)
  between operations  0.64 us (3%)
    pallas_call x1, Pallas kernels, local(): pl.pallas_call(functools.partial(reduce_kernel, dims), out_shape=(jax.Sha...  22.6 us
    pallas_call x1, Pallas kernels, local(): pl.pallas_call(functools.partial(basis_kernel, dims), out_shape=(jax.Shap...  1.69 us

profile of v2, /device:TPU:0, one launch (start us, length us, event | category | flops | bytes accessed | tf_op | source)
XLA Modules:
  0.0 25.0 jit_solution(9113908591695790722)
XLA Ops:
  0.6 22.6 %reduce.1 = (f32[1280,128]{1,0:T(8,128)S(1)}, bf16[1,1280,128]{2,1,0:T(8,128)(2,1)S(1)}, f32[64,64]{1,0:T(8,128)S(1)}, f32[2,2]{1,0:T(2,128)S(1)}) custom-call(f32[1280,128]{1,0:T(8,128)} %bitcast.3, s32[8,512]{1,0:T(8,128)} %nbr_hbm.1, f32[8,512]{1,0:T(8,128)} %w_hbm.1, f32[2,2]{1,0:T(2,128)} %coupling_hbm.1), custom_call_target="tpu_custom_call" | custom-call | tf_op jit(solution)/shard_map/reduce/pallas_call | solution.py:231
  23.3 1.7 %basis.1 = (f32[1280,128]{1,0:T(8,128)}, f32[1280,128]{1,0:T(8,128)}) custom-call(f32[64,64]{1,0:T(8,128)S(1)} %get-tuple-element.8.inv_ref, f32[1280,128]{1,0:T(8,128)S(1)} %get-tuple-element.9.res_ref, bf16[1,1280,128]{2,1,0:T(8,128)(2,1)S(1)} %get-tuple-element.10.other_ref, f32[2,2]{1,0:T(2,128)S(1)} %get-tuple-element.11.coupling_ref), custom_call_target="tpu_custom_call" | custom-call | tf_op jit(solution)/shard_map/basis/pallas_call | solution.py:259

commit v3 on v2

--- a/solution.py
+++ b/solution.py
@@ -118,6 +118,27 @@
     def part(q, d, block):
         return jnp.dot(block, stencil[q, d * LANES:(d + 1) * LANES, :], preferred_element_type=F32)
 
+    rows = snaps * fields
+    highs, lows = [None] * chunks, [None] * chunks
+    res_copies = []
+    early = 1
+
+    def send_res(q):
+        for d in range(1, grps):
+            at = pl.ds(q * rows, rows)
+            copy = pltpu.make_async_remote_copy(
+                src_ref=resbf.at[at], dst_ref=other_ref.at[d - 1, at],
+                send_sem=s3.at[d - 1, q], recv_sem=r3.at[d - 1, q],
+                device_id=(me_t, lax.rem(me_g + d, grps)), device_id_type=MESH)
+            copy.start()
+            res_copies.append(copy)
+
+    def finish(q, stencil_sum):
+        res = chunk(q) - stencil_sum
+        res_ref[q * rows:(q + 1) * rows, :] = res
+        highs[q], lows[q] = split(res)
+        resbf[q * rows:(q + 1) * rows, :] = highs[q]
+
     sums = []
     for q in range(chunks):
         total = None
@@ -126,19 +147,14 @@
                 term = part(q, d, own[q + d - 1])
                 total = term if total is None else total + term
         sums.append(total)
+    for q in range(1, chunks - 1):
+        finish(q, sums[q])
+        if q == early:
+            send_res(q)
     for copy in sends:
         copy.wait()
-    sums[0] = sums[0] + part(0, 0, halo[0])
-    sums[-1] = sums[-1] + part(chunks - 1, 2, halo[1])
-    highs, lows = [], []
-    rows = snaps * fields
-    for q in range(chunks):
-        res = chunk(q) - sums[q]
-        res_ref[q * rows:(q + 1) * rows, :] = res
-        high, low_part = split(res)
-        resbf[q * rows:(q + 1) * rows, :] = high
-        highs.append(high)
-        lows.append(low_part)
+    finish(0, sums[0] + part(0, 0, halo[0]))
+    finish(chunks - 1, sums[-1] + part(chunks - 1, 2, halo[1]))
 
     gram = jnp.zeros((2 * snaps, snaps), F32)
     for f in range(fields):
@@ -162,14 +178,16 @@
             copies.append(copy)
         return copies
 
+    total = gsend[...]
     copies = exchange(n1, near, gsend, grecv, s1, r1)
-    total = gsend[...]
+    for q in range(chunks):
+        if q != early:
+            send_res(q)
     for d, copy in enumerate(copies):
         copy.wait_recv()
         total = total + grecv[d]
     tsend[...] = total
     far_copies = exchange(n2, far, tsend, trecv, s2, r2)
-    res_copies = exchange(grps, lambda d: (me_t, lax.rem(me_g + d, grps)), resbf, other_ref, s3, r3)
     for d, copy in enumerate(far_copies):
         copy.wait_recv()
         total = total + trecv[d]
@@ -249,7 +267,7 @@
             pltpu.VMEM((n1 - 1, snaps // 2, 2 * snaps), F32),
             pltpu.VMEM((snaps // 2, 2 * snaps), F32),
             pltpu.VMEM((n2 - 1, snaps // 2, 2 * snaps), F32),
-            dma(2), dma(2), dma(n1 - 1), dma(n1 - 1), dma(n2 - 1), dma(n2 - 1), dma(grps - 1), dma(grps - 1),
+            dma(2), dma(2), dma(n1 - 1), dma(n1 - 1), dma(n2 - 1), dma(n2 - 1), pltpu.SemaphoreType.DMA((grps - 1, chunks)), pltpu.SemaphoreType.DMA((grps - 1, chunks)),
             dma(4),
         ],
         compiler_params=pltpu.CompilerParams(

time: 25.2 us -> 22.5 us (0.89)
  Pallas kernels: 24.3 us -> 21.7 us
    pallas_call x1, Pallas kernels: 22.6 us -> 20 us  [local(): pl.pallas_call(functools.partial(reduce_kernel, dims), out_shape=(jax.Sha...]
where the time goes in v3:
time: 22.5 us; the launch traced here: 22.3 us
  Pallas kernels  21.7 us (96%)
  between operations  0.64 us (3%)
    pallas_call x1, Pallas kernels, local(): pl.pallas_call(functools.partial(reduce_kernel, dims), out_shape=(jax.Sha...  20 us
    pallas_call x1, Pallas kernels, local(): pl.pallas_call(functools.partial(basis_kernel, dims), out_shape=(jax.Shap...  1.69 us

profile of v3, /device:TPU:0, one launch (start us, length us, event | category | flops | bytes accessed | tf_op | source)
XLA Modules:
  0.0 22.3 jit_solution(2043924416560238463)
XLA Ops:
  0.6 20.0 %reduce.1 = (f32[1280,128]{1,0:T(8,128)S(1)}, bf16[1,1280,128]{2,1,0:T(8,128)(2,1)S(1)}, f32[64,64]{1,0:T(8,128)S(1)}, f32[2,2]{1,0:T(2,128)S(1)}) custom-call(f32[1280,128]{1,0:T(8,128)} %bitcast.3, s32[8,512]{1,0:T(8,128)} %nbr_hbm.1, f32[8,512]{1,0:T(8,128)} %w_hbm.1, f32[2,2]{1,0:T(2,128)} %coupling_hbm.1), custom_call_target="tpu_custom_call" | custom-call | tf_op jit(solution)/shard_map/reduce/pallas_call | solution.py:249
  20.6 1.7 %basis.1 = (f32[1280,128]{1,0:T(8,128)}, f32[1280,128]{1,0:T(8,128)}) custom-call(f32[64,64]{1,0:T(8,128)S(1)} %get-tuple-element.8.inv_ref, f32[1280,128]{1,0:T(8,128)S(1)} %get-tuple-element.9.res_ref, bf16[1,1280,128]{2,1,0:T(8,128)(2,1)S(1)} %get-tuple-element.10.other_ref, f32[2,2]{1,0:T(2,128)S(1)} %get-tuple-element.11.coupling_ref), custom_call_target="tpu_custom_call" | custom-call | tf_op jit(solution)/shard_map/basis/pallas_call | solution.py:277

commit v4 on v3

--- a/solution.py
+++ b/solution.py
@@ -91,16 +91,6 @@
         return jnp.concatenate(
             [x_ref[pl.ds(f * chunks + q, snaps, stride=step), :] for f in range(fields)], axis=0)
 
-    ins[1].wait()
-    ins[2].wait()
-    iota = lax.broadcasted_iota(jnp.int32, (3 * LANES, LANES), 0)
-    for q in range(chunks):
-        here = slice(q * LANES, (q + 1) * LANES)
-        total = jnp.zeros((3 * LANES, LANES), F32)
-        for j in range(nbr_ref.shape[0]):
-            total = total + jnp.where(iota == nbr_ref[j:j + 1, here] - q * LANES, w_ref[j:j + 1, here], 0.0)
-        stencil[q] = total.astype(BF16)
-
     ins[0].wait()
     edge[0] = chunk(chunks - 1).astype(BF16)
     edge[1] = chunk(0).astype(BF16)
@@ -112,6 +102,16 @@
             device_id=(to, me_g), device_id_type=MESH)
         copy.start()
         sends.append(copy)
+
+    ins[1].wait()
+    ins[2].wait()
+    iota = lax.broadcasted_iota(jnp.int32, (3 * LANES, LANES), 0)
+    for q in range(chunks):
+        here = slice(q * LANES, (q + 1) * LANES)
+        total = jnp.zeros((3 * LANES, LANES), F32)
+        for j in range(nbr_ref.shape[0]):
+            total = total + jnp.where(iota == nbr_ref[j:j + 1, here] - q * LANES, w_ref[j:j + 1, here], 0.0)
+        stencil[q] = total.astype(BF16)
 
     own = [chunk(q).astype(BF16) for q in range(chunks)]
 
@@ -201,7 +201,7 @@
         copy.wait()
 
 
-def basis_kernel(dims, inv_ref, res_ref, other_ref, coupling_ref, basis_ref, coupled_ref):
+def basis_kernel(dims, inv_ref, res_ref, other_ref, coupling_ref, basis_hbm, coupled_hbm, basis_ref, coupled_ref, sems):
     tiles, grps, low, snaps, fields, chunks = dims
     me_g = lax.axis_index("grp")
     rows, step = snaps * fields, fields * chunks
@@ -218,20 +218,26 @@
 
     own_scale = scale(0)
     scales = [scale(d) for d in range(1, grps)]
-    for f in range(fields):
-        for q in range(chunks):
-            at = pl.ds(q * rows + f * snaps, snaps)
-            to = pl.ds(f * chunks + q, snaps, stride=step)
-            rh, rl = split(res_ref[at, :])
-            basis = jnp.dot(three, jnp.concatenate([rh, rh, rl], axis=0), preferred_element_type=F32)
-            basis_ref[to, :] = basis
-            rounded = basis.astype(BF16).astype(F32)
-            mixed = own_scale * rounded
-            for d in range(1, grps):
-                there = other_ref[d - 1, at, :]
-                theirs = jnp.dot(two, jnp.concatenate([there, there], axis=0), preferred_element_type=F32)
-                mixed = mixed + scales[d - 1] * theirs.astype(BF16).astype(F32)
-            coupled_ref[to, :] = rounded + mixed
+    places = [(pl.ds(q * rows + f * snaps, snaps), pl.ds(f * chunks + q, snaps, stride=step))
+              for f in range(fields) for q in range(chunks)]
+    for at, to in places:
+        rh, rl = split(res_ref[at, :])
+        basis = jnp.dot(three, jnp.concatenate([rh, rh, rl], axis=0), preferred_element_type=F32)
+        basis_ref[to, :] = basis
+    first = pltpu.make_async_copy(basis_ref, basis_hbm, sems.at[0])
+    first.start()
+    for at, to in places:
+        rounded = basis_ref[to, :].astype(BF16).astype(F32)
+        mixed = own_scale * rounded
+        for d in range(1, grps):
+            there = other_ref[d - 1, at, :]
+            theirs = jnp.dot(two, jnp.concatenate([there, there], axis=0), preferred_element_type=F32)
+            mixed = mixed + scales[d - 1] * theirs.astype(BF16).astype(F32)
+        coupled_ref[to, :] = rounded + mixed
+    second = pltpu.make_async_copy(coupled_ref, coupled_hbm, sems.at[1])
+    second.start()
+    first.wait()
+    second.wait()
 
 
 def local(mesh, snapshots, neighbors, weights, coupling):
@@ -278,7 +284,8 @@
         functools.partial(basis_kernel, dims),
         out_shape=(jax.ShapeDtypeStruct((count, LANES), F32),) * 2,
         in_specs=[vmem] * 4,
-        out_specs=(vmem,) * 2,
+        out_specs=(pl.BlockSpec(memory_space=pltpu.HBM),) * 2,
+        scratch_shapes=[pltpu.VMEM((count, LANES), F32), pltpu.VMEM((count, LANES), F32), dma(2)],
         compiler_params=pltpu.CompilerParams(vmem_limit_bytes=32 * 2 ** 20),
         name="basis",
     )(inverse, res, other, pairs)

time: 22.5 us -> 22.4 us (level)
  no operation moved by 1% of the time
where the time goes in v4:
time: 22.4 us; the launch traced here: 22.3 us
  Pallas kernels  21.6 us (96%)
  between operations  0.64 us (3%)
    pallas_call x1, Pallas kernels, local(): pl.pallas_call(functools.partial(reduce_kernel, dims), out_shape=(jax.Sha...  20 us
    pallas_call x1, Pallas kernels, local(): pl.pallas_call(functools.partial(basis_kernel, dims), out_shape=(jax.Shap...  1.65 us

profile of v4, /device:TPU:0, one launch (start us, length us, event | category | flops | bytes accessed | tf_op | source)
XLA Modules:
  0.0 22.3 jit_solution(3705329970961477828)
XLA Ops:
  0.6 20.0 %reduce.1 = (f32[1280,128]{1,0:T(8,128)S(1)}, bf16[1,1280,128]{2,1,0:T(8,128)(2,1)S(1)}, f32[64,64]{1,0:T(8,128)S(1)}, f32[2,2]{1,0:T(2,128)S(1)}) custom-call(f32[1280,128]{1,0:T(8,128)} %bitcast.3, s32[8,512]{1,0:T(8,128)} %nbr_hbm.1, f32[8,512]{1,0:T(8,128)} %w_hbm.1, f32[2,2]{1,0:T(2,128)} %coupling_hbm.1), custom_call_target="tpu_custom_call" | custom-call | tf_op jit(solution)/shard_map/reduce/pallas_call | solution.py:255
  20.6 1.6 %basis.1 = (f32[1280,128]{1,0:T(8,128)}, f32[1280,128]{1,0:T(8,128)}) custom-call(f32[64,64]{1,0:T(8,128)S(1)} %get-tuple-element.8.inv_ref, f32[1280,128]{1,0:T(8,128)S(1)} %get-tuple-element.9.res_ref, bf16[1,1280,128]{2,1,0:T(8,128)(2,1)S(1)} %get-tuple-element.10.other_ref, f32[2,2]{1,0:T(2,128)S(1)} %get-tuple-element.11.coupling_ref), custom_call_target="tpu_custom_call" | custom-call | tf_op jit(solution)/shard_map/basis/pallas_call | solution.py:283

commit v5 on v4

--- a/solution.py
+++ b/solution.py
@@ -151,18 +151,24 @@
         finish(q, sums[q])
         if q == early:
             send_res(q)
+
+    def products(which):
+        total = jnp.zeros((2 * snaps, snaps), F32)
+        for f in range(fields):
+            at = slice(f * snaps, (f + 1) * snaps)
+            high = jnp.concatenate([highs[q][at] for q in which], axis=1)
+            low_part = jnp.concatenate([lows[q][at] for q in which], axis=1)
+            total = total + lax.dot_general(jnp.concatenate([high, low_part], axis=0), high,
+                                            (((1,), (1,)), ((), ())), preferred_element_type=F32)
+        return total
+
+    inner = products(list(range(1, chunks - 1)))
     for copy in sends:
         copy.wait()
     finish(0, sums[0] + part(0, 0, halo[0]))
     finish(chunks - 1, sums[-1] + part(chunks - 1, 2, halo[1]))
 
-    gram = jnp.zeros((2 * snaps, snaps), F32)
-    for f in range(fields):
-        at = slice(f * snaps, (f + 1) * snaps)
-        high = jnp.concatenate([h[at] for h in highs], axis=1)
-        low_part = jnp.concatenate([h[at] for h in lows], axis=1)
-        gram = gram + lax.dot_general(jnp.concatenate([high, low_part], axis=0), high,
-                                      (((1,), (1,)), ((), ())), preferred_element_type=F32)
+    gram = inner + products([0, chunks - 1])
     gram = gram[:snaps] + (gram[snaps:] + gram[snaps:].T)
     gram = gram * (1.0 / (fields * chunks * LANES * tiles * grps))
     half = snaps // 2

time: 22.4 us -> 22.2 us (level)
  no operation moved by 1% of the time
where the time goes in v5:
time: 22.2 us; the launch traced here: 22.1 us
  Pallas kernels  21.5 us (97%)
  between operations  0.64 us (3%)
    pallas_call x1, Pallas kernels, local(): pl.pallas_call(functools.partial(reduce_kernel, dims), out_shape=(jax.Sha...  19.8 us
    pallas_call x1, Pallas kernels, local(): pl.pallas_call(functools.partial(basis_kernel, dims), out_shape=(jax.Shap...  1.65 us

profile of v5, /device:TPU:0, one launch (start us, length us, event | category | flops | bytes accessed | tf_op | source)
XLA Modules:
  0.0 22.1 jit_solution(12001787033402096599)
XLA Ops:
  0.6 19.8 %reduce.1 = (f32[1280,128]{1,0:T(8,128)S(1)}, bf16[1,1280,128]{2,1,0:T(8,128)(2,1)S(1)}, f32[64,64]{1,0:T(8,128)S(1)}, f32[2,2]{1,0:T(2,128)S(1)}) custom-call(f32[1280,128]{1,0:T(8,128)} %bitcast.3, s32[8,512]{1,0:T(8,128)} %nbr_hbm.1, f32[8,512]{1,0:T(8,128)} %w_hbm.1, f32[2,2]{1,0:T(2,128)} %coupling_hbm.1), custom_call_target="tpu_custom_call" | custom-call | tf_op jit(solution)/shard_map/reduce/pallas_call | solution.py:261
  20.4 1.6 %basis.1 = (f32[1280,128]{1,0:T(8,128)}, f32[1280,128]{1,0:T(8,128)}) custom-call(f32[64,64]{1,0:T(8,128)S(1)} %get-tuple-element.8.inv_ref, f32[1280,128]{1,0:T(8,128)S(1)} %get-tuple-element.9.res_ref, bf16[1,1280,128]{2,1,0:T(8,128)(2,1)S(1)} %get-tuple-element.10.other_ref, f32[2,2]{1,0:T(2,128)S(1)} %get-tuple-element.11.coupling_ref), custom_call_target="tpu_custom_call" | custom-call | tf_op jit(solution)/shard_map/basis/pallas_call | solution.py:289
